TPU v7x, 32 devices: a whole 2x2x4 slice. The times are simulated.
32 devices in a mesh: ctx: 8 (over z, y), dp: 4 (over x, core).
Axes of the slice: x: 2, y: 2, z: 4, core: 2. Of those that a mesh axis runs over, the one named last changes fastest.
Arguments:
- queries: bfloat16 [4, 2048, 2048], P('dp', 'ctx'), may hold values from -9 to 9, as said below
- keys: bfloat16 [4, 2048, 512], P('dp', 'ctx'), may hold values from -9 to 9
- values: bfloat16 [4, 2048, 512], P('dp', 'ctx'), may hold values from -20 to 20
- hyena_x1: bfloat16 [4, 2048, 2048], P('dp', 'ctx'), may hold values from -6 to 6
- hyena_x2: bfloat16 [4, 2048, 2048], P('dp', 'ctx'), may hold values from -6 to 6
- hyena_v: bfloat16 [4, 2048, 2048], P('dp', 'ctx'), may hold values from -6 to 6
- filters: bfloat16 [128, 128], replicated, may hold values from -6 to 6
- panels: bfloat16 [4, 256, 4096], P('dp', 'ctx'), may hold values from -6 to 6
- owner: int32 [4, 256, 1], P('dp', 'ctx'), may hold values from 0 to 3; in each aligned block of 32 rows (0 to 31, 32 to 63, ..., all dimensions but the last counted through in order) at most 32 rows name the same one
- step_rows: int32 [4, 256], P('dp', 'ctx'), may hold values from 0 to 2047, as said below
Outputs:
- mixed: bfloat16 [4, 2048, 2048], P('dp', 'ctx')
Inputs may be any that keep to these rules, and one draw needn't show every extreme that they name: In the hidden draw a few queries are aligned with two earlier keys; the normal draw stays within 6. `step_rows`: the panels held by the device at index c of ctx belong to positions c * 256 to (c + 1) * 256 - 1 of their traces. Of the panels on one device, at most 32 have the same owner, and that bound is reached.
All inputs are finite; a program needn't handle non-finite values.
Results may differ from a plain program's by a relative error of at most 0.0055.
Values may be sent and summed in bfloat16 or wider, within the bound.
A program may use at most 128 MiB of HBM per device.

v0:
```python
import math

import jax
import jax.numpy as jnp
from jax import lax
from jax.sharding import PartitionSpec as P

HEADS = 16
KV_HEADS = 4
HEAD_DIM = 128


NEG = -1e30


def passed_along(block, axis, distance):
    devices = range(lax.axis_size(axis))
    route = [(i - distance, i) for i in devices if i - distance in devices]
    return lax.ppermute(block, axis, route)


def attend_block(state, query, q_pos, key_blk, val_blk, key_pos, scale):
    m_old, l_old, o_old = state
    scores = (
        jnp.einsum("rhgd,khd->hgrk", query, key_blk, preferred_element_type=jnp.float32) * scale
    )
    allowed = key_pos[None, :] <= q_pos[:, None]
    scores = jnp.where(allowed, scores, NEG)
    m_new = jnp.maximum(m_old, jnp.max(scores, axis=-1))
    expo = jnp.where(allowed, jnp.exp(scores - m_new[..., None]), jnp.float32(0.0))
    factor = jnp.exp(m_old - m_new)
    l_new = l_old * factor + jnp.sum(expo, axis=-1)
    o_new = o_old * factor[..., None] + jnp.einsum(
        "hgrk,khd->hgrd", expo.astype(jnp.bfloat16), val_blk, preferred_element_type=jnp.float32
    )
    return (m_new, l_new, o_new)


def fold_attention(groups, key_rows, val_rows):
    grp = HEADS // KV_HEADS
    scale = HEAD_DIM ** (-0.5)
    inits = []
    for query, q_pos in groups:
        count = query.shape[0]
        inits.append(
            (
                jnp.full((KV_HEADS, grp, count), NEG, jnp.float32),
                jnp.zeros((KV_HEADS, grp, count), jnp.float32),
                jnp.zeros((KV_HEADS, grp, count, HEAD_DIM), jnp.float32),
            )
        )

    def fold(carry, piece, start):
        key_piece, val_piece = piece
        length = key_piece.shape[0]
        blk = math.gcd(length, 512)
        key_piece = key_piece.reshape(length, KV_HEADS, HEAD_DIM)
        val_piece = val_piece.reshape(length, KV_HEADS, HEAD_DIM)
        results = []
        for (query, q_pos), state in zip(groups, carry):

            def run(current, query=query, q_pos=q_pos):

                def step(index, inner):
                    key_blk = lax.dynamic_slice_in_dim(key_piece, index * blk, blk, 0)
                    val_blk = lax.dynamic_slice_in_dim(val_piece, index * blk, blk, 0)
                    key_pos = index * blk + jnp.arange(blk, dtype=jnp.int32)
                    return attend_block(inner, query, q_pos, key_blk, val_blk, key_pos, scale)

                return lax.fori_loop(0, length // blk, step, current)

            def keep(current):
                return current

            results.append(lax.cond(start > jnp.max(q_pos), keep, run, state))
        return tuple(results)

    finals = fold(
        tuple(inits),
        (
            lax.all_gather(key_rows, "ctx", axis=0, tiled=True),
            lax.all_gather(val_rows, "ctx", axis=0, tiled=True),
        ),
        jnp.int32(0),
    )
    outputs = []
    for (query, q_pos), (m_fin, l_fin, o_fin) in zip(groups, finals):
        count = query.shape[0]
        normed = o_fin / l_fin[..., None]
        outputs.append(normed.transpose(2, 0, 1, 3).reshape(count, HEADS * HEAD_DIM))
    return outputs


def attention(query, key_rows, val_rows, tok, ctx_index):
    grp = HEADS // KV_HEADS
    query = query.reshape(tok, KV_HEADS, grp, HEAD_DIM)
    first = ctx_index * tok
    positions = first + jnp.arange(tok, dtype=jnp.int32)
    return fold_attention(((query, positions),), key_rows, val_rows)[0]


def hyena_conv(first_in, value_in, filters, tok):
    width = first_in.shape[1]
    taps = filters.shape[1]
    fgroups = filters.shape[0]
    u_rows = (first_in.astype(jnp.float32) * value_in.astype(jnp.float32)).astype(jnp.bfloat16)
    before = passed_along(u_rows[tok - taps :], "ctx", 1)
    extended = jnp.concatenate([before, u_rows], 0)
    nblk = tok // taps
    blocks = extended.reshape(nblk + 1, taps, fgroups, width // fgroups)
    rows_at = jnp.arange(taps, dtype=jnp.int32)
    lag = rows_at[:, None] - rows_at[None, :]
    wrapped = (lag + taps) % taps
    selector = (wrapped[None, :, :] == rows_at[:, None, None]).astype(jnp.bfloat16)
    circulant = jnp.einsum(
        "gk,kij->gij", filters, selector, preferred_element_type=jnp.float32
    ).astype(jnp.bfloat16)
    nothing = jnp.zeros((), jnp.bfloat16)
    lower = jnp.where((lag >= 0)[None], circulant, nothing)
    upper = jnp.where((lag < 0)[None], circulant, nothing)
    conv = jnp.einsum("gij,bjgc->bigc", lower, blocks[1:], preferred_element_type=jnp.float32)
    conv = conv + jnp.einsum(
        "gij,bjgc->bigc", upper, blocks[:-1], preferred_element_type=jnp.float32
    )
    return conv.reshape(tok, width)


def blend(rows, width):
    gates = rows[:, :width].astype(jnp.float32)
    vals = rows[:, width:].astype(jnp.float32)
    return (jax.nn.sigmoid(gates) * vals).astype(jnp.bfloat16)


def place_rows(slots, rows, total_slots):
    placing = (jnp.arange(total_slots, dtype=jnp.int32)[:, None] == slots[None, :]).astype(
        jnp.bfloat16
    )
    return jnp.dot(placing, rows, preferred_element_type=jnp.float32).astype(jnp.bfloat16)


def route_hints(panels, owner, step_rows, width, tok, ctx_index):
    dp_count = lax.axis_size("dp")
    count = panels.shape[1]
    entries = panels.shape[2]
    cap = min(count, 4 * count // dp_count)
    owners = owner[0, :, 0]
    marks = (owners[:, None] == jnp.arange(dp_count, dtype=jnp.int32)[None, :]).astype(jnp.int32)
    before_mask = (
        jnp.arange(count, dtype=jnp.int32)[:, None] > jnp.arange(count, dtype=jnp.int32)[None, :]
    ).astype(jnp.int32)
    earlier = jnp.sum(jnp.dot(before_mask, marks) * marks, axis=1)
    slots = owners * cap + earlier
    base_row = ctx_index * tok
    row_buffer = jnp.full((dp_count * cap,), base_row, jnp.int32).at[slots].set(step_rows[0])
    arrived_rows = (
        lax.all_to_all(
            row_buffer.reshape(dp_count, cap), "dp", split_axis=0, concat_axis=0, tiled=True
        ).reshape(dp_count * cap)
        - base_row
    )
    buffer = place_rows(slots, panels[0], dp_count * cap)
    received = lax.all_to_all(
        buffer.reshape(dp_count, cap, entries), "dp", split_axis=0, concat_axis=0, tiled=True
    )
    arrived = blend(received.reshape(dp_count * cap, entries), width)
    landing = (jnp.arange(tok, dtype=jnp.int32)[:, None] == arrived_rows[None, :]).astype(
        jnp.bfloat16
    )
    return jnp.dot(landing, arrived, preferred_element_type=jnp.float32)


def per_device(
    queries, keys, values, hyena_x1, hyena_x2, hyena_v, filters, panels, owner, step_rows
):
    tok = queries.shape[1]
    width = hyena_x1.shape[2]
    ctx_index = lax.axis_index("ctx")
    conv = hyena_conv(hyena_x1[0], hyena_v[0], filters, tok)
    attended = attention(queries[0], keys[0], values[0], tok, ctx_index)
    hints = route_hints(panels, owner, step_rows, width, tok, ctx_index)
    total = hyena_x2[0].astype(jnp.float32) * conv + attended + hints
    return total.astype(jnp.bfloat16)[None]


def solution(mesh):
    placed = (
        P("dp", "ctx", None),
        P("dp", "ctx", None),
        P("dp", "ctx", None),
        P("dp", "ctx", None),
        P("dp", "ctx", None),
        P("dp", "ctx", None),
        P(),
        P("dp", "ctx", None),
        P("dp", "ctx", None),
        P("dp", "ctx"),
    )
    return jax.shard_map(
        per_device, mesh=mesh, in_specs=placed, out_specs=P("dp", "ctx", None), check_vma=False
    )
```

profile of v0, /device:TPU:0, one launch (start us, length us, event | category | flops | bytes accessed | tf_op | source)
XLA Modules:
  0.0 208.6 jit_solution(9671920750449791751)
XLA Ops:
  6.5 1.9 copy.45
  8.5 1.8 copy.46
  10.3 1.6 multiply_convert_fusion
  12.0 0.9 slice_bitcast_fusion
  12.8 5.7 %collective-permute-start = (bf16[128,2048]{1,0:T(8,128)(2,1)}, bf16[128,2048]{1,0:T(8,128)(2,1)}, u32[]{:S(2)}, u32[]{:S(2)}) collective-permute-start(bf16[128,2048]{1,0:T(8,128)(2,1)} %slice_bitcast_fusion), channel_id=1, source_target_pairs={{0,4},{4,8},{8,12},{12,16},{16,20},{20,24},{24,28},{1,5},{5,9},{9,... | collective-permute-start | bytes 1572872 | tf_op jit(solution)/shard_map/ppermute | solution.py:19
  18.6 0.8 scatter_custom_fusion
  20.1 3.2 %all-to-all-start = ((s32[4,1,32]{2,1,0:T(1,128)}), s32[4,1,32]{2,1,0:T(1,128)S(1)}, u32[]{:S(2)}, u32[]{:S(2)}) async-start(s32[4,1,32]{2,1,0:T(1,128)} %bitcast.20), calls=%async_computation | async-start | bytes 4096 | tf_op jit(solution)/shard_map/all_to_all | solution.py:156
  23.4 1.4 convolution_convert_fusion
  24.8 10.4 %select_bitcast_fusion = (bf16[128,128,128,1]{0,2,1,3:T(8,128)(2,1)}, bf16[128,128,128,1]{0,2,1,3:T(8,128)(2,1)}) fusion(pred[128,128]{1,0:T(8,128)(4,1)S(1)} %get-tuple-element.239, pred[128,128]{1,0:T(8,128)(4,1)S(1)} %get-tuple-element.240, bf16[128,128]{1,0:T(8,128)(2,1)S(1)} %copy-done.8, s32[128,128]{1,0:T(8,128)S(1)} %add_select_fusion), kind=kOutput, calls=%fused_computation.29 | convolution fusion | flops 545259520 | bytes 8519680 | tf_op jit(solution)/shard_map/gk,kij->gij/dot_general | solution.py:115
  36.4 6.8 %copy.53 = bf16[128,128,128,1]{2,1,3,0:T(8,128)(2,1)} copy(bf16[128,128,128,1]{0,2,1,3:T(8,128)(2,1)} %get-tuple-element.238) | data formatting | bytes 8388608 | tf_op jit(solution)/shard_map/jit(_where)/select_n | solution.py:119
  43.1 1.1 convert_element_type.67
  44.2 5.0 %fusion.28 = f32[128,2,16,128]{3,2,1,0:T(8,128)S(1)} fusion(bf16[128,128,128,1]{2,1,3,0:T(8,128)(2,1)} %copy.53, bf16[2,128,128,16]{1,0,3,2:T(2,128)(2,1)} %convert_element_type.67), kind=kOutput, calls=%fused_computation.46 | convolution fusion | flops 134217728 | bytes 7340032 | tf_op jit(solution)/shard_map/gij,bjgc->bigc/dot_general | solution.py:121
  50.5 6.7 %copy.54 = bf16[128,128,128,1]{2,1,3,0:T(8,128)(2,1)} copy(bf16[128,128,128,1]{0,2,1,3:T(8,128)(2,1)} %get-tuple-element.237) | data formatting | bytes 8388608 | tf_op jit(solution)/shard_map/jit(_where)/select_n | solution.py:120
  57.3 4.3 %all-to-all-start.1 = ((bf16[4,32,4096]{2,1,0:T(8,128)(2,1)}), bf16[4,32,4096]{2,1,0:T(8,128)(2,1)}, u32[]{:S(2)}, u32[]{:S(2)}) async-start(bf16[4,32,4096]{2,1,0:T(8,128)(2,1)} %bitcast.105), calls=%async_computation.1 | async-start | bytes 2097152 | tf_op jit(solution)/shard_map/all_to_all | solution.py:162
  62.2 2.1 %pad_maximum_fusion = bf16[256,2048]{1,0:T(8,128)(2,1)} fusion(bf16[256,2048]{1,0:T(8,128)(2,1)S(1)} %bitcast.102, bf16[128,2048]{1,0:T(8,128)(2,1)} %collective-permute-done), kind=kLoop, calls=%fused_computation.44 | loop fusion | flops 2097152 | bytes 2621440 | tf_op jit(solution)/shard_map/concatenate | solution.py:108
  64.3 2.3 %copy.40 = bf16[256,2048]{0,1:T(8,128)(2,1)} copy(bf16[256,2048]{1,0:T(8,128)(2,1)} %pad_maximum_fusion) | data formatting | bytes 2097152 | tf_op jit(solution)/shard_map/slice | solution.py:123
  66.6 1.3 slice.23
  67.9 4.5 %add_bitcast_fusion = f32[2,128,128,16]{1,3,0,2:T(8,128)S(1)} fusion(f32[128,2,16,128]{3,2,1,0:T(8,128)S(1)} %fusion.28, bf16[128,128,128,1]{2,1,3,0:T(8,128)(2,1)} %copy.54, bf16[2,128,128,16]{1,0,3,2:T(2,128)(2,1)S(1)} %slice.23), kind=kOutput, calls=%fused_computation.40 | convolution fusion | flops 134742016 | bytes 9437184 | tf_op jit(solution)/shard_map/gij,bjgc->bigc/dot_general | solution.py:122
  72.4 1.1 copy.43
  73.6 1.9 copy.44
  75.5 43.8 %all-gather.7.cloned.1.call-done = bf16[1,2048,512]{1,2,0:T(8,128)(2,1)} async-done(((bf16[1,256,512]{1,2,0:T(8,128)(2,1)}), bf16[1,2048,512]{1,2,0:T(8,128)(2,1)}) %all-gather.7.cloned.1.call-update) | async-done | bytes 2097168 | tf_op jit(solution)/shard_map/all_gather | solution.py:82
  119.3 73.5 %conditional.1 = (f32[4,4,256]{2,1,0:T(4,128)}, f32[4,4,256,128]{3,2,1,0:T(8,128)S(1)}) conditional(s32[]{:T(128)} %convert_element_type.70, (bf16[2048,512]{0,1:T(8,128)(2,1)}, bf16[2048,512]{0,1:T(8,128)(2,1)}, bf16[1,256,2048]{2,1,0:T(8,128)(2,1)S(1)}, s32[256]{0:T(256)}) %tuple.66, () %tuple.28), branch_computations={%region_1.6_spmd, %region_6.7_spmd} | conditional | flops 1102729728 | bytes 70129024 | solution.py:75
  120.5 72.3 %while.17 = (s32[]{:T(128)}, f32[4,4,256]{2,1,0:T(4,128)S(1)}, f32[4,4,256]{2,1,0:T(4,128)}, f32[4,4,256,128]{3,2,1,0:T(8,128)S(1)}, s32[256]{0:T(256)}, /*index...) while((s32[]{:T(128)}, f32[4,4,256]{2,1,0:T(4,128)S(1)}, ...), condition=%wide.region_5.5_spmd.clone, body=%wide.region_2.4_spmd.clone.sunk | while | flops 1102729728 | bytes 65934604 | solution.py:70
  120.5 0.8 broadcast_compare_fusion.2
  121.4 6.4 %fusion.62 = (f32[4,4,256]{2,1,0:T(4,128)}, f32[4,512,256,4]{2,1,3,0:T(8,128)}) fusion(pred[256,512]{0,1:T(8,128)(4,1)S(1)} %broadcast_compare_fusion.2, bf16[256,4,4,128]{3,0,2,1:T(8,128)(2,1)S(1)} %get-tuple-element.328, bf16[2048,4,128]{0,2,1:T(8,128)(2,1)} %get-tuple-element.327, s32[]{:T(128)S(6)} %select_n.105), kind=kOutput, calls=%fused_computation.3.clone.1 | convolution fusion | flops 543158272 | bytes 10108932 | tf_op jit(solution)/shard_map/cond/branch_0_fun/while/body/eval_jaxpr/rhgd,khd->hgrk/dot_general | solution.py:25
  127.7 0.7 select_maximum_fusion.2
  128.5 4.6 %fusion.63 = f32[4,4,256]{2,1,0:T(4,128)S(1)} fusion(f32[4,512,256,4]{2,1,3,0:T(8,128)} %get-tuple-element.295, f32[4,4,256]{2,1,0:T(4,128)S(1)} %select_maximum_fusion.2, pred[256,512]{0,1:T(8,128)(4,1)S(1)} %broadcast_compare_fusion.2), kind=kLoop, calls=%fused_computation.5.clone.1 | loop fusion | flops 10481664 | bytes 8552448 | tf_op jit(solution)/shard_map/cond/branch_0_fun/while/body/eval_jaxpr/reduce_sum | solution.py:32
  133.2 1.2 copy-done.1
  134.3 4.2 %fusion.65 = f32[4,4,256,128]{3,2,1,0:T(8,128)S(1)} fusion(f32[4,4,256,128]{3,2,1,0:T(8,128)S(1)} %get-tuple-element.313, f32[4,512,256,4]{2,1,3,0:T(8,128)S(1)} %copy-done.1, f32[4,4,256]{2,1,0:T(4,128)S(1)} %select_maximum_fusion.2, pred[256,512]{0,1:T(8,128)(4,1)S(1)} %broadcast_compare_fusion.2, f32[4,4,256]{2,1,0:T(4,128)S(1)} %get-tuple-element.297, ...), kind=kOutput, calls=%fused_computation.9.clone.1 | convolution fusion | flops 548929536 | bytes 13271045 | tf_op jit(solution)/shard_map/cond/branch_0_fun/while/body/eval_jaxpr/hgrk,khd->hgrd/dot_general | solution.py:33
  138.6 0.8 broadcast_compare_fusion.2
  139.4 6.4 %fusion.62 = (f32[4,4,256]{2,1,0:T(4,128)}, f32[4,512,256,4]{2,1,3,0:T(8,128)}) fusion(pred[256,512]{0,1:T(8,128)(4,1)S(1)} %broadcast_compare_fusion.2, bf16[256,4,4,128]{3,0,2,1:T(8,128)(2,1)S(1)} %get-tuple-element.328, bf16[2048,4,128]{0,2,1:T(8,128)(2,1)} %get-tuple-element.327, s32[]{:T(128)S(6)} %select_n.105), kind=kOutput, calls=%fused_computation.3.clone.1 | convolution fusion | flops 543158272 | bytes 10108932 | tf_op jit(solution)/shard_map/cond/branch_0_fun/while/body/eval_jaxpr/rhgd,khd->hgrk/dot_general | solution.py:25
  146.6 4.6 %fusion.63 = f32[4,4,256]{2,1,0:T(4,128)S(1)} fusion(f32[4,512,256,4]{2,1,3,0:T(8,128)} %get-tuple-element.295, f32[4,4,256]{2,1,0:T(4,128)S(1)} %select_maximum_fusion.2, pred[256,512]{0,1:T(8,128)(4,1)S(1)} %broadcast_compare_fusion.2), kind=kLoop, calls=%fused_computation.5.clone.1 | loop fusion | flops 10481664 | bytes 8552448 | tf_op jit(solution)/shard_map/cond/branch_0_fun/while/body/eval_jaxpr/reduce_sum | solution.py:32
  151.2 1.2 copy-done.1
  152.4 4.2 %fusion.65 = f32[4,4,256,128]{3,2,1,0:T(8,128)S(1)} fusion(f32[4,4,256,128]{3,2,1,0:T(8,128)S(1)} %get-tuple-element.313, f32[4,512,256,4]{2,1,3,0:T(8,128)S(1)} %copy-done.1, f32[4,4,256]{2,1,0:T(4,128)S(1)} %select_maximum_fusion.2, pred[256,512]{0,1:T(8,128)(4,1)S(1)} %broadcast_compare_fusion.2, f32[4,4,256]{2,1,0:T(4,128)S(1)} %get-tuple-element.297, ...), kind=kOutput, calls=%fused_computation.9.clone.1 | convolution fusion | flops 548929536 | bytes 13271045 | tf_op jit(solution)/shard_map/cond/branch_0_fun/while/body/eval_jaxpr/hgrk,khd->hgrd/dot_general | solution.py:33
  156.7 0.8 broadcast_compare_fusion.2
  157.5 6.4 %fusion.62 = (f32[4,4,256]{2,1,0:T(4,128)}, f32[4,512,256,4]{2,1,3,0:T(8,128)}) fusion(pred[256,512]{0,1:T(8,128)(4,1)S(1)} %broadcast_compare_fusion.2, bf16[256,4,4,128]{3,0,2,1:T(8,128)(2,1)S(1)} %get-tuple-element.328, bf16[2048,4,128]{0,2,1:T(8,128)(2,1)} %get-tuple-element.327, s32[]{:T(128)S(6)} %select_n.105), kind=kOutput, calls=%fused_computation.3.clone.1 | convolution fusion | flops 543158272 | bytes 10108932 | tf_op jit(solution)/shard_map/cond/branch_0_fun/while/body/eval_jaxpr/rhgd,khd->hgrk/dot_general | solution.py:25
  164.6 4.6 %fusion.63 = f32[4,4,256]{2,1,0:T(4,128)S(1)} fusion(f32[4,512,256,4]{2,1,3,0:T(8,128)} %get-tuple-element.295, f32[4,4,256]{2,1,0:T(4,128)S(1)} %select_maximum_fusion.2, pred[256,512]{0,1:T(8,128)(4,1)S(1)} %broadcast_compare_fusion.2), kind=kLoop, calls=%fused_computation.5.clone.1 | loop fusion | flops 10481664 | bytes 8552448 | tf_op jit(solution)/shard_map/cond/branch_0_fun/while/body/eval_jaxpr/reduce_sum | solution.py:32
  169.3 1.2 copy-done.1
  170.5 4.2 %fusion.65 = f32[4,4,256,128]{3,2,1,0:T(8,128)S(1)} fusion(f32[4,4,256,128]{3,2,1,0:T(8,128)S(1)} %get-tuple-element.313, f32[4,512,256,4]{2,1,3,0:T(8,128)S(1)} %copy-done.1, f32[4,4,256]{2,1,0:T(4,128)S(1)} %select_maximum_fusion.2, pred[256,512]{0,1:T(8,128)(4,1)S(1)} %broadcast_compare_fusion.2, f32[4,4,256]{2,1,0:T(4,128)S(1)} %get-tuple-element.297, ...), kind=kOutput, calls=%fused_computation.9.clone.1 | convolution fusion | flops 548929536 | bytes 13271045 | tf_op jit(solution)/shard_map/cond/branch_0_fun/while/body/eval_jaxpr/hgrk,khd->hgrd/dot_general | solution.py:33
  174.7 0.8 broadcast_compare_fusion.2
  175.6 6.4 %fusion.62 = (f32[4,4,256]{2,1,0:T(4,128)}, f32[4,512,256,4]{2,1,3,0:T(8,128)}) fusion(pred[256,512]{0,1:T(8,128)(4,1)S(1)} %broadcast_compare_fusion.2, bf16[256,4,4,128]{3,0,2,1:T(8,128)(2,1)S(1)} %get-tuple-element.328, bf16[2048,4,128]{0,2,1:T(8,128)(2,1)} %get-tuple-element.327, s32[]{:T(128)S(6)} %select_n.105), kind=kOutput, calls=%fused_computation.3.clone.1 | convolution fusion | flops 543158272 | bytes 10108932 | tf_op jit(solution)/shard_map/cond/branch_0_fun/while/body/eval_jaxpr/rhgd,khd->hgrk/dot_general | solution.py:25
  182.7 4.6 %fusion.63 = f32[4,4,256]{2,1,0:T(4,128)S(1)} fusion(f32[4,512,256,4]{2,1,3,0:T(8,128)} %get-tuple-element.295, f32[4,4,256]{2,1,0:T(4,128)S(1)} %select_maximum_fusion.2, pred[256,512]{0,1:T(8,128)(4,1)S(1)} %broadcast_compare_fusion.2), kind=kLoop, calls=%fused_computation.5.clone.1 | loop fusion | flops 10481664 | bytes 8552448 | tf_op jit(solution)/shard_map/cond/branch_0_fun/while/body/eval_jaxpr/reduce_sum | solution.py:32
  187.4 1.2 copy-done.1
  188.5 4.2 %fusion.65 = f32[4,4,256,128]{3,2,1,0:T(8,128)S(1)} fusion(f32[4,4,256,128]{3,2,1,0:T(8,128)S(1)} %get-tuple-element.313, f32[4,512,256,4]{2,1,3,0:T(8,128)S(1)} %copy-done.1, f32[4,4,256]{2,1,0:T(4,128)S(1)} %select_maximum_fusion.2, pred[256,512]{0,1:T(8,128)(4,1)S(1)} %broadcast_compare_fusion.2, f32[4,4,256]{2,1,0:T(4,128)S(1)} %get-tuple-element.297, ...), kind=kOutput, calls=%fused_computation.9.clone.1 | convolution fusion | flops 548929536 | bytes 13271045 | tf_op jit(solution)/shard_map/cond/branch_0_fun/while/body/eval_jaxpr/hgrk,khd->hgrd/dot_general | solution.py:33
  192.8 1.4 divide_bitcast_fusion
  194.2 1.4 copy.48
  195.6 1.9 reshape.139
  197.5 4.3 %fusion.24 = bf16[1,256,2048]{2,1,0:T(8,128)(2,1)} fusion(f32[256,2048]{1,0:T(8,128)} %reshape.139, f32[256,2048]{1,0:T(8,128)} %copy.44, bf16[1,256,2048]{2,1,0:T(8,128)(2,1)S(1)} %copy-done.7, bf16[128,4096]{1,0:T(8,128)(2,1)} %bitcast.23, s32[128]{0:T(128)S(1)} %copy-done.6), kind=kOutput, calls=%fused_computation.35 | convolution fusion | flops 138706944 | bytes 7340544 | tf_op jit(solution)/shard_map/dot_general | solution.py:169
  (74 shorter events, 7.1 us)
Async XLA Ops:
  6.5 16.9 %copy-start = (bf16[1,32,4096]{2,1,0:T(8,128)(2,1)S(1)}, bf16[1,32,4096]{2,1,0:T(8,128)(2,1)}, u32[]{:S(2)}) copy-start(bf16[1,32,4096]{2,1,0:T(8,128)(2,1)} %param.21) | copy-start | bytes 786436
  6.5 3.8 %copy-start.2 = (bf16[1,256,2048]{2,1,0:T(8,128)(2,1)S(1)}, bf16[1,256,2048]{2,1,0:T(8,128)(2,1)}, u32[]{:S(2)}) copy-start(bf16[1,256,2048]{2,1,0:T(8,128)(2,1)} %param.19) | copy-start | bytes 3145732
  6.5 69.0 %all-gather.5.cloned.1.call-start = ((), (), s32[]{:S(2)}) async-start(), calls=%async_computation.2 | async-start | bytes 2359296 | tf_op jit(solution)/shard_map/all_gather | solution.py:81
  8.5 110.8 %all-gather.7.cloned.1.call-start = ((), (), s32[]{:S(2)}) async-start(), calls=%async_computation.3 | async-start | bytes 2359296 | tf_op jit(solution)/shard_map/all_gather | solution.py:82
  10.3 8.2 %copy-start.9 = (s32[1,32,1]{1,2,0:T(1,128)S(1)}, s32[1,32,1]{1,2,0:T(1,128)}, u32[]{:S(2)}) copy-start(s32[1,32,1]{1,2,0:T(1,128)} %param.22) | copy-start | bytes 388
  10.3 14.5 %copy-start.8 = (bf16[128,128]{1,0:T(8,128)(2,1)S(1)}, bf16[128,128]{1,0:T(8,128)(2,1)}, u32[]{:S(2)}) copy-start(bf16[128,128]{1,0:T(8,128)(2,1)} %param.20) | copy-start | bytes 98308
  12.8 49.4 %collective-permute-start = (bf16[128,2048]{1,0:T(8,128)(2,1)}, bf16[128,2048]{1,0:T(8,128)(2,1)}, u32[]{:S(2)}, u32[]{:S(2)}) collective-permute-start(bf16[128,2048]{1,0:T(8,128)(2,1)} %slice_bitcast_fusion), channel_id=1, source_target_pairs={{0,4},{4,8},{8,12},{12,16},{16,20},{20,24},{24,28},{1,5},{5,9},{9,... | collective-permute-start | bytes 1572872 | tf_op jit(solution)/shard_map/ppermute | solution.py:19
  20.1 37.1 %all-to-all-start = ((s32[4,1,32]{2,1,0:T(1,128)}), s32[4,1,32]{2,1,0:T(1,128)S(1)}, u32[]{:S(2)}, u32[]{:S(2)}) async-start(s32[4,1,32]{2,1,0:T(1,128)} %bitcast.20), calls=%async_computation | async-start | bytes 4096 | tf_op jit(solution)/shard_map/all_to_all | solution.py:156
  57.3 140.2 %all-to-all-start.1 = ((bf16[4,32,4096]{2,1,0:T(8,128)(2,1)}), bf16[4,32,4096]{2,1,0:T(8,128)(2,1)}, u32[]{:S(2)}, u32[]{:S(2)}) async-start(bf16[4,32,4096]{2,1,0:T(8,128)(2,1)} %bitcast.105), calls=%async_computation.1 | async-start | bytes 2097152 | tf_op jit(solution)/shard_map/all_to_all | solution.py:162
  73.6 45.6 %copy-start.3 = (bf16[1,256,2048]{2,1,0:T(8,128)(2,1)S(1)}, bf16[1,256,2048]{2,1,0:T(8,128)(2,1)}, u32[]{:S(2)}) copy-start(bf16[1,256,2048]{2,1,0:T(8,128)(2,1)} %param.14) | copy-start | bytes 3145732
  128.5 4.6 %copy-start.4 = (f32[4,4,256]{2,1,0:T(4,128)S(1)}, f32[4,4,256]{2,1,0:T(4,128)}, u32[]{:S(2)}) copy-start(f32[4,4,256]{2,1,0:T(4,128)} %get-tuple-element.312) | copy-start | bytes 49156 | tf_op jit(solution)/shard_map/cond/branch_0_fun/while
  128.5 5.9 %copy-start.1 = (f32[4,512,256,4]{2,1,3,0:T(8,128)S(1)}, f32[4,512,256,4]{2,1,3,0:T(8,128)}, u32[]{:S(2)}) copy-start(f32[4,512,256,4]{2,1,3,0:T(8,128)} %get-tuple-element.295) | copy-start | bytes 25165828 | tf_op jit(solution)/shard_map/cond/branch_0_fun/while
  133.1 5.4 %copy-start.5 = (f32[4,4,256]{2,1,0:T(4,128)}, f32[4,4,256]{2,1,0:T(4,128)S(1)}, u32[]{:S(2)}) copy-start(f32[4,4,256]{2,1,0:T(4,128)S(1)} %get-tuple-element.324) | copy-start | bytes 49156 | tf_op jit(solution)/shard_map/cond/branch_0_fun/while
  146.5 4.6 %copy-start.4 = (f32[4,4,256]{2,1,0:T(4,128)S(1)}, f32[4,4,256]{2,1,0:T(4,128)}, u32[]{:S(2)}) copy-start(f32[4,4,256]{2,1,0:T(4,128)} %get-tuple-element.312) | copy-start | bytes 49156 | tf_op jit(solution)/shard_map/cond/branch_0_fun/while
  146.5 5.9 %copy-start.1 = (f32[4,512,256,4]{2,1,3,0:T(8,128)S(1)}, f32[4,512,256,4]{2,1,3,0:T(8,128)}, u32[]{:S(2)}) copy-start(f32[4,512,256,4]{2,1,3,0:T(8,128)} %get-tuple-element.295) | copy-start | bytes 25165828 | tf_op jit(solution)/shard_map/cond/branch_0_fun/while
  151.2 5.4 %copy-start.5 = (f32[4,4,256]{2,1,0:T(4,128)}, f32[4,4,256]{2,1,0:T(4,128)S(1)}, u32[]{:S(2)}) copy-start(f32[4,4,256]{2,1,0:T(4,128)S(1)} %get-tuple-element.324) | copy-start | bytes 49156 | tf_op jit(solution)/shard_map/cond/branch_0_fun/while
  164.6 4.6 %copy-start.4 = (f32[4,4,256]{2,1,0:T(4,128)S(1)}, f32[4,4,256]{2,1,0:T(4,128)}, u32[]{:S(2)}) copy-start(f32[4,4,256]{2,1,0:T(4,128)} %get-tuple-element.312) | copy-start | bytes 49156 | tf_op jit(solution)/shard_map/cond/branch_0_fun/while
  164.6 5.9 %copy-start.1 = (f32[4,512,256,4]{2,1,3,0:T(8,128)S(1)}, f32[4,512,256,4]{2,1,3,0:T(8,128)}, u32[]{:S(2)}) copy-start(f32[4,512,256,4]{2,1,3,0:T(8,128)} %get-tuple-element.295) | copy-start | bytes 25165828 | tf_op jit(solution)/shard_map/cond/branch_0_fun/while
  169.3 5.4 %copy-start.5 = (f32[4,4,256]{2,1,0:T(4,128)}, f32[4,4,256]{2,1,0:T(4,128)S(1)}, u32[]{:S(2)}) copy-start(f32[4,4,256]{2,1,0:T(4,128)S(1)} %get-tuple-element.324) | copy-start | bytes 49156 | tf_op jit(solution)/shard_map/cond/branch_0_fun/while
  182.7 4.6 %copy-start.4 = (f32[4,4,256]{2,1,0:T(4,128)S(1)}, f32[4,4,256]{2,1,0:T(4,128)}, u32[]{:S(2)}) copy-start(f32[4,4,256]{2,1,0:T(4,128)} %get-tuple-element.312) | copy-start | bytes 49156 | tf_op jit(solution)/shard_map/cond/branch_0_fun/while
  182.7 5.9 %copy-start.1 = (f32[4,512,256,4]{2,1,3,0:T(8,128)S(1)}, f32[4,512,256,4]{2,1,3,0:T(8,128)}, u32[]{:S(2)}) copy-start(f32[4,512,256,4]{2,1,3,0:T(8,128)} %get-tuple-element.295) | copy-start | bytes 25165828 | tf_op jit(solution)/shard_map/cond/branch_0_fun/while
  187.4 5.4 %copy-start.5 = (f32[4,4,256]{2,1,0:T(4,128)}, f32[4,4,256]{2,1,0:T(4,128)S(1)}, u32[]{:S(2)}) copy-start(f32[4,4,256]{2,1,0:T(4,128)S(1)} %get-tuple-element.324) | copy-start | bytes 49156 | tf_op jit(solution)/shard_map/cond/branch_0_fun/while
  195.6 1.9 copy-start.6
  195.6 1.9 copy-start.7
Sparse Core Ops, SparseCore 0:
  9.4 58.4 all-gather.4
  70.0 49.2 all-gather.6
where the time goes:
time: 210 us; the launch traced here: 209 us
  matrix products  68 us (32%)
  waiting for transfers between devices  43.8 us (21%)
  local copies, waits for them, and re-layouts  37.7 us (18%)
  other arithmetic  31.2 us (15%)
  between operations  14.2 us (7%)
  starting transfers between devices  13.2 us (6%)
    all_gather x1, waiting for transfers between devices, fold_attention(): lax.all_gather(val_rows, 'ctx', axis=0, tiled=True)  43.8 us
    dot_general x4, matrix products, attend_block(): jnp.einsum('rhgd,khd->hgrk', query, key_blk, preferred_element_type=jnp.f...  25.6 us
    reduce_sum x4, other arithmetic, attend_block(): l_new = l_old * factor + jnp.sum(expo, axis=-1)  18.5 us
    dot_general x4, matrix products, attend_block(): jnp.einsum('hgrk,khd->hgrd', expo.astype(jnp.bfloat16), val_blk, preferre...  16.8 us
    dot_general x1, matrix products, hyena_conv(): jnp.einsum('gk,kij->gij', filters, selector, preferred_element_type=jnp.f...  10.4 us
    select_n x1, local copies, waits for them, and re-layouts, hyena_conv(): lower = jnp.where((lag >= 0)[None], circulant, nothing)  6.78 us
    select_n x1, local copies, waits for them, and re-layouts, hyena_conv(): upper = jnp.where((lag < 0)[None], circulant, nothing)  6.74 us
    ppermute x1, starting transfers between devices, passed_along(): return lax.ppermute(block, axis, route)  5.65 us
  transfers between devices with their start and end apart: 5, of which 1 were waited for; matrix products, arithmetic and copies ran while one was open for 60% of the time, Pallas kernels for 0%

commit v1 on v0

v1 whole, which is shorter than its diff:
```python
import functools
import math

import jax
import jax.numpy as jnp
from jax import lax
from jax.experimental import pallas as pl
from jax.experimental.pallas import tpu as pltpu
from jax.sharding import PartitionSpec as P

HEAD_DIM = 128
LANES = 128
NEG = -1e30
MESH = pl.DeviceIdType.MESH
F32 = jnp.float32
BF16 = jnp.bfloat16


def kernel(
    n_ctx, n_dp,
    q_ref, k_ref, v_ref, x1_ref, x2_ref, hv_ref, filt_ref, pan_ref, own_ref, step_ref,
    out_ref,
    kv, uext, hfwd, hint, code, toep, conv, m_ref, l_ref, o_ref,
    zsend, zrecv, ysend, yrecv, hsend, hrecv, csend, crecv,
):
    tok, width = q_ref.shape
    kv_width = k_ref.shape[1]
    heads = width // HEAD_DIM
    kv_heads = kv_width // HEAD_DIM
    grp = heads // kv_heads
    fgroups, taps = filt_ref.shape
    chan = width // fgroups
    count = pan_ref.shape[0]
    seq = tok * n_ctx
    n_z = n_ctx // 2
    c = lax.axis_index("ctx")
    d = lax.axis_index("dp")
    z = c // 2
    y = c % 2
    low = y == 0
    high = y == 1
    has_up = z < n_z - 1
    has_down = z > 0
    partner = (2 * z + 1 - y, d)
    up = (jnp.minimum(c + 2, n_ctx - 1), d)
    down = (jnp.maximum(c - 2, 0), d)

    barrier = pltpu.get_barrier_semaphore()
    pl.semaphore_signal(barrier, 1, device_id=partner, device_id_type=MESH)
    for s in range(1, n_dp):
        pl.semaphore_signal(barrier, 1, device_id=(c, (d + s) % n_dp), device_id_type=MESH)

    @pl.when(has_up)
    def _():
        pl.semaphore_signal(barrier, 1, device_id=up, device_id_type=MESH)

    @pl.when(has_down)
    def _():
        pl.semaphore_signal(barrier, 1, device_id=down, device_id_type=MESH)

    kv[c, :, :kv_width] = k_ref[...]
    kv[c, :, kv_width:] = v_ref[...]
    uext[taps:, :] = x1_ref[...] * hv_ref[...]

    @pl.when(c == 0)
    def _():
        uext[:taps, :] = jnp.zeros((taps, width), BF16)

    pl.semaphore_wait(
        barrier, n_dp + has_up.astype(jnp.int32) + has_down.astype(jnp.int32)
    )

    def remote(src, dst, s_sem, r_sem, who):
        return pltpu.make_async_remote_copy(
            src_ref=src, dst_ref=dst, send_sem=s_sem, recv_sem=r_sem,
            device_id=who, device_id_type=MESH,
        )

    def z_copy(hi):
        slot = kv.at[2 * hi + y]
        return remote(slot, slot, zsend.at[hi], zrecv.at[hi], up)

    def z_extra_block(hi):
        slot = kv.at[2 * hi]
        return remote(slot, slot, zsend.at[n_z], zrecv.at[n_z], up)

    halo_out = uext.at[pl.ds(tok, taps)]
    halo_in = uext.at[pl.ds(0, taps)]

    def z_extra_halo():
        return remote(hfwd, halo_in, zsend.at[n_z], zrecv.at[n_z], up)

    def y_copy(hi):
        slot = kv.at[2 * hi + y]
        return remote(slot, slot, ysend.at[hi], yrecv.at[hi], partner)

    def y_arrival(hi):
        slot = kv.at[2 * hi + 1 - y]
        return remote(slot, slot, ysend.at[hi], yrecv.at[hi], partner)

    def y_halo_low():
        return remote(halo_out, halo_in, ysend.at[n_z], yrecv.at[n_z], partner)

    def y_halo_high():
        return remote(halo_out, hfwd, ysend.at[n_z], yrecv.at[n_z], partner)

    @pl.when(has_up)
    def _():
        z_copy(z).start()

    @pl.when(low)
    def _():
        y_copy(z).start()

    @pl.when(high & has_up)
    def _():
        y_halo_high().start()

    half = pan_ref.shape[1] // 2
    gates = pan_ref[:, :half].astype(F32)
    hint[d] = (jax.nn.sigmoid(gates) * pan_ref[:, half:].astype(F32)).astype(BF16)
    eye = lax.broadcasted_iota(jnp.int32, (count, count), 0) == lax.broadcasted_iota(
        jnp.int32, (count, count), 1
    )
    steps = jnp.sum(
        jnp.where(eye, jnp.broadcast_to(step_ref[...], (count, count)), 0), axis=1, keepdims=True
    )
    code[d] = jnp.broadcast_to(own_ref[...] * seq + steps, (count, LANES))

    def hint_copy(s, me):
        return remote(
            hint.at[me], hint.at[me], hsend.at[s], hrecv.at[s], (c, (d + s) % n_dp)
        )

    def code_copy(s, me):
        return remote(
            code.at[me], code.at[me], csend.at[s], crecv.at[s], (c, (d + s) % n_dp)
        )

    for s in range(1, n_dp):
        hint_copy(s, d).start()
        code_copy(s, d).start()

    factor = HEAD_DIM ** -0.5 * math.log2(math.e)

    def attend(slot, diagonal=False):
        def one(kh, carry):
            k_at = pl.ds(pl.multiple_of(kh * HEAD_DIM, HEAD_DIM), HEAD_DIM)
            v_at = pl.ds(pl.multiple_of(kv_width + kh * HEAD_DIM, HEAD_DIM), HEAD_DIM)
            key = kv[slot, :, k_at]
            val = kv[slot, :, v_at]
            for g in range(grp):
                h = kh * grp + g
                query = q_ref[:, pl.ds(pl.multiple_of(h * HEAD_DIM, HEAD_DIM), HEAD_DIM)]
                score = lax.dot_general(
                    key, query, (((1,), (1,)), ((), ())), preferred_element_type=F32
                ) * factor
                if diagonal:
                    keep = lax.broadcasted_iota(jnp.int32, (tok, tok), 0) <= (
                        lax.broadcasted_iota(jnp.int32, (tok, tok), 1)
                    )
                    score = jnp.where(keep, score, NEG)
                    top = jnp.max(score, axis=0, keepdims=True)
                else:
                    before = m_ref[h]
                    top = jnp.maximum(before, jnp.max(score, axis=0, keepdims=True))
                expo = jnp.exp2(score - top)
                total = jnp.sum(expo, axis=0, keepdims=True)
                part = lax.dot_general(
                    val, expo.astype(BF16), (((0,), (0,)), ((), ())), preferred_element_type=F32
                )
                if diagonal:
                    l_ref[h] = total
                    o_ref[h] = part
                else:
                    shrink = jnp.exp2(before - top)
                    l_ref[h] = l_ref[h] * shrink + total
                    o_ref[h] = o_ref[h] * shrink + part
                m_ref[h] = top
            return carry

        lax.fori_loop(0, kv_heads, one, 0)

    attend(c, diagonal=True)

    lag_at = lax.broadcasted_iota(jnp.int32, (taps, 2 * taps), 0)
    col_at = lax.broadcasted_iota(jnp.int32, (taps, 2 * taps), 1)
    flip = jnp.where(lag_at == taps - col_at, 1.0, 0.0).astype(BF16)
    per_tile = LANES // chan
    n_tiles = width // LANES
    lane_group = lax.broadcasted_iota(jnp.int32, (taps, LANES), 1) // chan
    n_blk = tok // taps

    def pick(prod, col):
        res = prod[:taps, col]
        for g in range(1, per_tile):
            res = jnp.where(lane_group == g, prod[g * taps:(g + 1) * taps, col], res)
        return res

    def conv_tile(tile, carry):
        at = pl.ds(pl.multiple_of(tile * LANES, LANES), LANES)
        rows = filt_ref[pl.ds(pl.multiple_of(tile * per_tile, per_tile), per_tile), :]
        first = jnp.dot(rows, flip, preferred_element_type=F32)
        for g in range(per_tile):
            row = jnp.broadcast_to(first[g:g + 1, :], (taps, 2 * taps))
            toep[tile, g * taps:(g + 1) * taps, :] = pltpu.roll(
                row, 0, 1, stride=1, stride_axis=0
            ).astype(BF16)
        lower = toep[tile, :, taps:]
        prod = jnp.dot(lower, uext[taps:2 * taps, at], preferred_element_type=F32)
        conv[:taps, at] = pick(prod, slice(None))
        for b in range(1, n_blk):
            prod = jnp.dot(
                toep[tile], uext[b * taps:(b + 2) * taps, at], preferred_element_type=F32
            )
            conv[b * taps:(b + 1) * taps, at] = pick(prod, slice(None))
        return carry

    lax.fori_loop(0, n_tiles, conv_tile, 0)

    @pl.when(low)
    def _():
        y_halo_low().start()

    @pl.when(high)
    def _():
        y_arrival(z).wait_recv()
        attend(2 * z)

    def step(k, carry):
        hi = z - k
        z_copy(hi).wait_recv()

        @pl.when(has_up)
        def _():
            z_copy(hi).start()

        @pl.when(high | (k >= 2))
        def _():
            y_copy(hi).start()

        attend(2 * hi + y)

        @pl.when((k >= 2) & (low | (k >= 3)))
        def _():
            y_arrival(hi + 1).wait_recv()
            attend(2 * (hi + 1) + 1 - y)

        return carry

    lax.fori_loop(1, z + 1, step, 0)

    @pl.when(low & has_up)
    def _():
        y_halo_high().wait_recv()
        z_extra_halo().start()

    @pl.when(high & has_up)
    def _():
        z_extra_block(z).start()

    def conv_halo():
        def tile_step(tile, carry):
            at = pl.ds(pl.multiple_of(tile * LANES, LANES), LANES)
            prod = jnp.dot(
                toep[tile, :, :taps], uext[:taps, at], preferred_element_type=F32
            )
            conv[:taps, at] += pick(prod, slice(None))
            return carry

        lax.fori_loop(0, n_tiles, tile_step, 0)

    @pl.when(high)
    def _():
        y_halo_low().wait_recv()
        conv_halo()

    @pl.when((low & (z >= 1)) | (z >= 2))
    def _():
        y_arrival(0).wait_recv()
        attend(1 - y)

    @pl.when(low & has_down)
    def _():
        z_extra_halo().wait_recv()
        conv_halo()

    @pl.when(high & has_down)
    def _():
        z_extra_block(z - 1).wait_recv()
        attend(2 * (z - 1))

    for s in range(1, n_dp):
        hint_copy(s, (d + n_dp - s) % n_dp).wait_recv()
        code_copy(s, (d + n_dp - s) % n_dp).wait_recv()

    spot = lax.broadcasted_iota(jnp.int32, (n_dp * count, tok), 1) + (d * seq + c * tok)
    codes = code[...].reshape(n_dp * count, LANES)[:, :1]
    landing = jnp.where(codes == spot, 1.0, 0.0).astype(BF16)
    for h in range(heads):
        at = pl.ds(h * HEAD_DIM, HEAD_DIM)
        placed = lax.dot_general(
            landing, hint[:, :, at].reshape(n_dp * count, HEAD_DIM),
            (((0,), (0,)), ((), ())), preferred_element_type=F32,
        )
        normed = (o_ref[h] / l_ref[h]).T
        out_ref[:, at] = (x2_ref[:, at].astype(F32) * conv[:, at] + normed + placed).astype(BF16)

    for s in range(1, n_dp):
        hint_copy(s, d).wait_send()
        code_copy(s, d).wait_send()

    @pl.when(low)
    def _():
        y_copy(z).wait_send()
        y_halo_low().wait_send()

    @pl.when(high & has_up)
    def _():
        y_halo_high().wait_send()
        z_extra_block(z).wait_send()

    @pl.when(low & has_up)
    def _():
        z_extra_halo().wait_send()

    @pl.when(has_up)
    def _():
        z_copy(z).wait_send()

    def drain(k, carry):
        @pl.when(has_up)
        def _():
            z_copy(z - k).wait_send()

        @pl.when(high | (k >= 2))
        def _():
            y_copy(z - k).wait_send()

        return carry

    lax.fori_loop(1, z + 1, drain, 0)


def solution(mesh):
    n_ctx, n_dp = mesh.shape["ctx"], mesh.shape["dp"]

    def per_device(q, k, v, x1, x2, hv, filters, panels, owner, step_rows):
        tok, width = q.shape[1:]
        kv_width = k.shape[2]
        heads = width // HEAD_DIM
        fgroups, taps = filters.shape
        count = panels.shape[1]
        n_z = n_ctx // 2
        dma = pltpu.SemaphoreType.DMA
        vmem = pl.BlockSpec(memory_space=pltpu.VMEM)
        out = pl.pallas_call(
            functools.partial(kernel, n_ctx, n_dp),
            out_shape=jax.ShapeDtypeStruct((tok, width), BF16),
            in_specs=[vmem] * 10,
            out_specs=vmem,
            scratch_shapes=[
                pltpu.VMEM((n_ctx, tok, 2 * kv_width), BF16),
                pltpu.VMEM((taps + tok, width), BF16),
                pltpu.VMEM((taps, width), BF16),
                pltpu.VMEM((n_dp, count, width), BF16),
                pltpu.VMEM((n_dp, count, LANES), jnp.int32),
                pltpu.VMEM((width // LANES, taps * fgroups * LANES // width, 2 * taps), BF16),
                pltpu.VMEM((tok, width), F32),
                pltpu.VMEM((heads, 1, tok), F32),
                pltpu.VMEM((heads, 1, tok), F32),
                pltpu.VMEM((heads, HEAD_DIM, tok), F32),
                dma((n_z + 1,)), dma((n_z + 1,)), dma((n_z + 1,)), dma((n_z + 1,)),
                dma((n_dp,)), dma((n_dp,)), dma((n_dp,)), dma((n_dp,)),
            ],
            compiler_params=pltpu.CompilerParams(
                collective_id=0, has_side_effects=True, vmem_limit_bytes=56 * 2**20
            ),
        )(q[0], k[0], v[0], x1[0], x2[0], hv[0], filters, panels[0], owner[0], step_rows)
        return out[None]

    rows = P("dp", "ctx", None)
    return jax.shard_map(
        per_device,
        mesh=mesh,
        in_specs=(rows,) * 6 + (P(), rows, rows, P("dp", "ctx")),
        out_specs=rows,
        check_vma=False,
    )
```

time: 210 us -> 80.2 us (0.38)
  the two profiles are of different devices: /device:TPU:0 before, /device:TPU:30 now
where the time goes in v1:
time: 80.2 us; the launch traced here: 80.1 us
  Pallas kernels  76.4 us (95%)
  local copies, waits for them, and re-layouts  3.65 us (5%)
    pallas_call x1, Pallas kernels, per_device(): pl.pallas_call(functools.partial(kernel, n_ctx, n_dp), out_shape=jax.Shap...  76.4 us
    unnamed x3, local copies, waits for them, and re-layouts  2.96 us

profile of v1, /device:TPU:30, one launch (start us, length us, event | category | flops | bytes accessed | tf_op | source)
XLA Modules:
  0.0 80.1 jit_solution(314404225301886475)
XLA Ops:
  0.0 0.0 copy-start
  0.0 0.7 copy-done
  0.7 0.7 copy.11.own_ref
  1.3 76.4 %shard_map.100 = bf16[256,2048]{1,0:T(8,128)(2,1)} custom-call(bf16[256,2048]{1,0:T(8,128)(2,1)} %bitcast.10, bf16[256,512]{1,0:T(8,128)(2,1)} %bitcast.14, bf16[256,512]{1,0:T(8,128)(2,1)} %bitcast.15, bf16[256,2048]{1,0:T(8,128)(2,1)} %bitcast.11, bf16[256,2048]{1,0:T(8,128)(2,1)} %bitcast.12, bf16[256,2048]{1,0:T(8,128)(2,1)} %bitcast.13, ...), custom_call_target="tpu_custom_call" | custom-call | tf_op jit(solution)/shard_map/pallas_call | solution.py:357
  77.8 2.3 %copy.13 = bf16[1,256,2048]{2,1,0:T(8,128)(2,1)} copy(bf16[1,256,2048]{2,1,0:T(8,128)(2,1)} %bitcast.9) | data formatting | bytes 2097152
Async XLA Ops:
  0.0 0.7 copy-start

commit v2 on v1

--- a/solution.py
+++ b/solution.py
@@ -11,6 +11,7 @@
 HEAD_DIM = 128
 LANES = 128
 NEG = -1e30
+CHUNKS = 2
 MESH = pl.DeviceIdType.MESH
 F32 = jnp.float32
 BF16 = jnp.bfloat16
@@ -18,13 +19,15 @@
 
 def kernel(
     n_ctx, n_dp,
-    q_ref, k_ref, v_ref, x1_ref, x2_ref, hv_ref, filt_ref, pan_ref, own_ref, step_ref,
+    q_hbm, k_hbm, v_hbm, x1_hbm, x2_hbm, hv_hbm, filt_ref, pan_hbm, own_ref, step_ref,
     out_ref,
+    q_ref, x1_ref, x2_ref, hv_ref, pan_ref,
     kv, uext, hfwd, hint, code, toep, conv, m_ref, l_ref, o_ref,
-    zsend, zrecv, ysend, yrecv, hsend, hrecv, csend, crecv,
+    zsend, zrecv, ysend, yrecv, hsend, hrecv, csend, crecv, load_sem,
 ):
     tok, width = q_ref.shape
-    kv_width = k_ref.shape[1]
+    kv_width = k_hbm.shape[1]
+    part_width = kv_width // CHUNKS
     heads = width // HEAD_DIM
     kv_heads = kv_width // HEAD_DIM
     grp = heads // kv_heads
@@ -58,9 +61,30 @@
     def _():
         pl.semaphore_signal(barrier, 1, device_id=down, device_id_type=MESH)
 
-    kv[c, :, :kv_width] = k_ref[...]
-    kv[c, :, kv_width:] = v_ref[...]
-    uext[taps:, :] = x1_ref[...] * hv_ref[...]
+    def load(src, dst, index):
+        return pltpu.make_async_copy(src, dst, load_sem.at[index])
+
+    own_loads = []
+    for ch in range(CHUNKS):
+        cols = pl.ds(ch * part_width, part_width)
+        own_loads.append((
+            load(k_hbm.at[:, cols], kv.at[c * CHUNKS + ch, :, pl.ds(0, part_width)], 2 * ch),
+            load(
+                v_hbm.at[:, cols], kv.at[c * CHUNKS + ch, :, pl.ds(part_width, part_width)],
+                2 * ch + 1,
+            ),
+        ))
+    at_sem = 2 * CHUNKS
+    load_x1 = load(x1_hbm, x1_ref, at_sem)
+    load_hv = load(hv_hbm, hv_ref, at_sem + 1)
+    load_pan = load(pan_hbm, pan_ref, at_sem + 2)
+    load_q = load(q_hbm, q_ref, at_sem + 3)
+    load_x2 = load(x2_hbm, x2_ref, at_sem + 4)
+    for pair in own_loads:
+        for one_load in pair:
+            one_load.start()
+    for one_load in (load_x1, load_hv, load_pan, load_q, load_x2):
+        one_load.start()
 
     @pl.when(c == 0)
     def _():
@@ -76,46 +100,60 @@
             device_id=who, device_id_type=MESH,
         )
 
-    def z_copy(hi):
-        slot = kv.at[2 * hi + y]
-        return remote(slot, slot, zsend.at[hi], zrecv.at[hi], up)
-
-    def z_extra_block(hi):
-        slot = kv.at[2 * hi]
-        return remote(slot, slot, zsend.at[n_z], zrecv.at[n_z], up)
+    def z_copy(hi, ch):
+        slot = kv.at[(2 * hi + y) * CHUNKS + ch]
+        at = hi * CHUNKS + ch
+        return remote(slot, slot, zsend.at[at], zrecv.at[at], up)
+
+    last = n_z * CHUNKS
+
+    def z_extra_block(hi, ch):
+        slot = kv.at[2 * hi * CHUNKS + ch]
+        return remote(slot, slot, zsend.at[last + ch], zrecv.at[last + ch], up)
 
     halo_out = uext.at[pl.ds(tok, taps)]
     halo_in = uext.at[pl.ds(0, taps)]
 
     def z_extra_halo():
-        return remote(hfwd, halo_in, zsend.at[n_z], zrecv.at[n_z], up)
-
-    def y_copy(hi):
-        slot = kv.at[2 * hi + y]
-        return remote(slot, slot, ysend.at[hi], yrecv.at[hi], partner)
-
-    def y_arrival(hi):
-        slot = kv.at[2 * hi + 1 - y]
-        return remote(slot, slot, ysend.at[hi], yrecv.at[hi], partner)
+        return remote(hfwd, halo_in, zsend.at[last], zrecv.at[last], up)
+
+    def y_copy(hi, ch):
+        slot = kv.at[(2 * hi + y) * CHUNKS + ch]
+        at = hi * CHUNKS + ch
+        return remote(slot, slot, ysend.at[at], yrecv.at[at], partner)
+
+    def y_arrival(hi, ch):
+        slot = kv.at[(2 * hi + 1 - y) * CHUNKS + ch]
+        at = hi * CHUNKS + ch
+        return remote(slot, slot, ysend.at[at], yrecv.at[at], partner)
 
     def y_halo_low():
-        return remote(halo_out, halo_in, ysend.at[n_z], yrecv.at[n_z], partner)
+        return remote(halo_out, halo_in, ysend.at[last], yrecv.at[last], partner)
 
     def y_halo_high():
-        return remote(halo_out, hfwd, ysend.at[n_z], yrecv.at[n_z], partner)
-
-    @pl.when(has_up)
-    def _():
-        z_copy(z).start()
-
-    @pl.when(low)
-    def _():
-        y_copy(z).start()
+        return remote(halo_out, hfwd, ysend.at[last], yrecv.at[last], partner)
+
+    for ch in range(CHUNKS):
+        for one_load in own_loads[ch]:
+            one_load.wait()
+
+        @pl.when(has_up)
+        def _():
+            z_copy(z, ch).start()
+
+        @pl.when(low)
+        def _():
+            y_copy(z, ch).start()
+
+    load_x1.wait()
+    load_hv.wait()
+    uext[taps:, :] = x1_ref[...] * hv_ref[...]
 
     @pl.when(high & has_up)
     def _():
         y_halo_high().start()
 
+    load_pan.wait()
     half = pan_ref.shape[1] // 2
     gates = pan_ref[:, :half].astype(F32)
     hint[d] = (jax.nn.sigmoid(gates) * pan_ref[:, half:].astype(F32)).astype(BF16)
@@ -143,14 +181,18 @@
 
     factor = HEAD_DIM ** -0.5 * math.log2(math.e)
 
-    def attend(slot, diagonal=False):
+    part_heads = kv_heads // CHUNKS
+
+    def attend(block, ch, diagonal=False):
+        slot = block * CHUNKS + ch
+
         def one(kh, carry):
             k_at = pl.ds(pl.multiple_of(kh * HEAD_DIM, HEAD_DIM), HEAD_DIM)
-            v_at = pl.ds(pl.multiple_of(kv_width + kh * HEAD_DIM, HEAD_DIM), HEAD_DIM)
+            v_at = pl.ds(pl.multiple_of(part_width + kh * HEAD_DIM, HEAD_DIM), HEAD_DIM)
             key = kv[slot, :, k_at]
             val = kv[slot, :, v_at]
             for g in range(grp):
-                h = kh * grp + g
+                h = (ch * part_heads + kh) * grp + g
                 query = q_ref[:, pl.ds(pl.multiple_of(h * HEAD_DIM, HEAD_DIM), HEAD_DIM)]
                 score = lax.dot_general(
                     key, query, (((1,), (1,)), ((), ())), preferred_element_type=F32
@@ -179,9 +221,15 @@
                 m_ref[h] = top
             return carry
 
-        lax.fori_loop(0, kv_heads, one, 0)
-
-    attend(c, diagonal=True)
+        lax.fori_loop(0, part_heads, one, 0)
+
+    load_q.wait()
+    for ch in range(CHUNKS):
+        attend(c, ch, diagonal=True)
+
+    @pl.when(low)
+    def _():
+        y_halo_low().start()
 
     lag_at = lax.broadcasted_iota(jnp.int32, (taps, 2 * taps), 0)
     col_at = lax.broadcasted_iota(jnp.int32, (taps, 2 * taps), 1)
@@ -216,39 +264,34 @@
             conv[b * taps:(b + 1) * taps, at] = pick(prod, slice(None))
         return carry
 
-    lax.fori_loop(0, n_tiles, conv_tile, 0)
-
-    @pl.when(low)
-    def _():
-        y_halo_low().start()
-
-    @pl.when(high)
-    def _():
-        y_arrival(z).wait_recv()
-        attend(2 * z)
-
-    def step(k, carry):
-        hi = z - k
-        z_copy(hi).wait_recv()
+    def step(i, carry):
+        hi = z - 1 - i // CHUNKS
+        ch = i % CHUNKS
+        z_copy(hi, ch).wait_recv()
 
         @pl.when(has_up)
         def _():
-            z_copy(hi).start()
-
-        @pl.when(high | (k >= 2))
-        def _():
-            y_copy(hi).start()
-
-        attend(2 * hi + y)
-
-        @pl.when((k >= 2) & (low | (k >= 3)))
-        def _():
-            y_arrival(hi + 1).wait_recv()
-            attend(2 * (hi + 1) + 1 - y)
-
+            z_copy(hi, ch).start()
+
+        @pl.when(high | (i >= CHUNKS))
+        def _():
+            y_copy(hi, ch).start()
+
+        attend(2 * hi + y, ch)
+
+        @pl.when((i >= 2 * CHUNKS) | (high & (i < CHUNKS)) | (low & (i >= CHUNKS)))
+        def _():
+            y_arrival(hi + 1, ch).wait_recv()
+            attend(2 * (hi + 1) + 1 - y, ch)
+
+        lax.fori_loop(i * n_tiles // (CHUNKS * z), (i + 1) * n_tiles // (CHUNKS * z), conv_tile, 0)
         return carry
 
-    lax.fori_loop(1, z + 1, step, 0)
+    lax.fori_loop(0, CHUNKS * z, step, 0)
+
+    @pl.when(z == 0)
+    def _():
+        lax.fori_loop(0, n_tiles, conv_tile, 0)
 
     @pl.when(low & has_up)
     def _():
@@ -257,7 +300,12 @@
 
     @pl.when(high & has_up)
     def _():
-        z_extra_block(z).start()
+        for ch in range(CHUNKS):
+            @pl.when(z == 0)
+            def _():
+                y_arrival(z, ch).wait_recv()
+
+            z_extra_block(z, ch).start()
 
     def conv_halo():
         def tile_step(tile, carry):
@@ -275,10 +323,14 @@
         y_halo_low().wait_recv()
         conv_halo()
 
-    @pl.when((low & (z >= 1)) | (z >= 2))
-    def _():
-        y_arrival(0).wait_recv()
-        attend(1 - y)
+    @pl.when((low & (z >= 1)) | (high & (z != 1)))
+    def _():
+        for ch in range(CHUNKS):
+            @pl.when(z > 0)
+            def _():
+                y_arrival(0, ch).wait_recv()
+
+            attend(1 - y, ch)
 
     @pl.when(low & has_down)
     def _():
@@ -287,13 +339,15 @@
 
     @pl.when(high & has_down)
     def _():
-        z_extra_block(z - 1).wait_recv()
-        attend(2 * (z - 1))
+        for ch in range(CHUNKS):
+            z_extra_block(z - 1, ch).wait_recv()
+            attend(2 * (z - 1), ch)
 
     for s in range(1, n_dp):
         hint_copy(s, (d + n_dp - s) % n_dp).wait_recv()
         code_copy(s, (d + n_dp - s) % n_dp).wait_recv()
 
+    load_x2.wait()
     spot = lax.broadcasted_iota(jnp.int32, (n_dp * count, tok), 1) + (d * seq + c * tok)
     codes = code[...].reshape(n_dp * count, LANES)[:, :1]
     landing = jnp.where(codes == spot, 1.0, 0.0).astype(BF16)
@@ -312,13 +366,15 @@
 
     @pl.when(low)
     def _():
-        y_copy(z).wait_send()
+        for ch in range(CHUNKS):
+            y_copy(z, ch).wait_send()
         y_halo_low().wait_send()
 
     @pl.when(high & has_up)
     def _():
         y_halo_high().wait_send()
-        z_extra_block(z).wait_send()
+        for ch in range(CHUNKS):
+            z_extra_block(z, ch).wait_send()
 
     @pl.when(low & has_up)
     def _():
@@ -326,20 +382,24 @@
 
     @pl.when(has_up)
     def _():
-        z_copy(z).wait_send()
-
-    def drain(k, carry):
+        for ch in range(CHUNKS):
+            z_copy(z, ch).wait_send()
+
+    def drain(i, carry):
+        hi = z - 1 - i // CHUNKS
+        ch = i % CHUNKS
+
         @pl.when(has_up)
         def _():
-            z_copy(z - k).wait_send()
-
-        @pl.when(high | (k >= 2))
-        def _():
-            y_copy(z - k).wait_send()
+            z_copy(hi, ch).wait_send()
+
+        @pl.when(high | (i >= CHUNKS))
+        def _():
+            y_copy(hi, ch).wait_send()
 
         return carry
 
-    lax.fori_loop(1, z + 1, drain, 0)
+    lax.fori_loop(0, CHUNKS * z, drain, 0)
 
 
 def solution(mesh):
@@ -351,16 +411,18 @@
         heads = width // HEAD_DIM
         fgroups, taps = filters.shape
         count = panels.shape[1]
-        n_z = n_ctx // 2
+        n_sem = (n_ctx // 2 + 1) * CHUNKS
         dma = pltpu.SemaphoreType.DMA
+        hbm = pl.BlockSpec(memory_space=pl.ANY)
         vmem = pl.BlockSpec(memory_space=pltpu.VMEM)
         out = pl.pallas_call(
             functools.partial(kernel, n_ctx, n_dp),
             out_shape=jax.ShapeDtypeStruct((tok, width), BF16),
-            in_specs=[vmem] * 10,
+            in_specs=[hbm] * 6 + [vmem, hbm, vmem, vmem],
             out_specs=vmem,
-            scratch_shapes=[
-                pltpu.VMEM((n_ctx, tok, 2 * kv_width), BF16),
+            scratch_shapes=[pltpu.VMEM((tok, width), BF16)] * 4 + [
+                pltpu.VMEM((count, panels.shape[2]), BF16),
+                pltpu.VMEM((n_ctx * CHUNKS, tok, 2 * kv_width // CHUNKS), BF16),
                 pltpu.VMEM((taps + tok, width), BF16),
                 pltpu.VMEM((taps, width), BF16),
                 pltpu.VMEM((n_dp, count, width), BF16),
@@ -370,8 +432,8 @@
                 pltpu.VMEM((heads, 1, tok), F32),
                 pltpu.VMEM((heads, 1, tok), F32),
                 pltpu.VMEM((heads, HEAD_DIM, tok), F32),
-                dma((n_z + 1,)), dma((n_z + 1,)), dma((n_z + 1,)), dma((n_z + 1,)),
-                dma((n_dp,)), dma((n_dp,)), dma((n_dp,)), dma((n_dp,)),
+                dma((n_sem,)), dma((n_sem,)), dma((n_sem,)), dma((n_sem,)),
+                dma((n_dp,)), dma((n_dp,)), dma((n_dp,)), dma((n_dp,)), dma((2 * CHUNKS + 5,)),
             ],
             compiler_params=pltpu.CompilerParams(
                 collective_id=0, has_side_effects=True, vmem_limit_bytes=56 * 2**20

time: 80.2 us -> 66.5 us (0.83)
  Pallas kernels: 76.4 us -> 62.6 us
    pallas_call x1, Pallas kernels: 76.4 us -> 62.6 us  [per_device(): pl.pallas_call(functools.partial(kernel, n_ctx, n_dp), out_shape=jax.Shap...]
where the time goes in v2:
time: 66.5 us; the launch traced here: 66.3 us
  Pallas kernels  62.6 us (94%)
  local copies, waits for them, and re-layouts  3.65 us (5%)
    pallas_call x1, Pallas kernels, per_device(): pl.pallas_call(functools.partial(kernel, n_ctx, n_dp), out_shape=jax.Shap...  62.6 us
    unnamed x3, local copies, waits for them, and re-layouts  2.96 us

profile of v2, /device:TPU:30, one launch (start us, length us, event | category | flops | bytes accessed | tf_op | source)
XLA Modules:
  0.0 66.3 jit_solution(13044645025515025503)
XLA Ops:
  0.0 0.0 copy-start
  0.0 0.7 copy-done
  0.7 0.7 %copy.11.own_ref = s32[32,1]{1,0:T(8,128)} copy(s32[32,1]{0,1:T(1,128)S(1)} %bitcast.17) | data formatting | bytes 256 | tf_op jit(solution)/shard_map/squeeze | solution.py:441
  1.3 62.6 %shard_map.100 = bf16[256,2048]{1,0:T(8,128)(2,1)} custom-call(bf16[256,2048]{1,0:T(8,128)(2,1)} %bitcast.10, bf16[256,512]{1,0:T(8,128)(2,1)} %bitcast.14, bf16[256,512]{1,0:T(8,128)(2,1)} %bitcast.15, bf16[256,2048]{1,0:T(8,128)(2,1)} %bitcast.11, bf16[256,2048]{1,0:T(8,128)(2,1)} %bitcast.12, bf16[256,2048]{1,0:T(8,128)(2,1)} %bitcast.13, ...), custom_call_target="tpu_custom_call" | custom-call | tf_op jit(solution)/shard_map/pallas_call | solution.py:418
  64.0 2.3 %copy.13 = bf16[1,256,2048]{2,1,0:T(8,128)(2,1)} copy(bf16[1,256,2048]{2,1,0:T(8,128)(2,1)} %bitcast.9) | data formatting | bytes 2097152
Async XLA Ops:
  0.0 0.7 copy-start
